TPU v7x, 512 devices: a whole 4x8x8 slice. The times are simulated.
512 devices in a mesh: tm: 16 (over x, z_hi, core), cell: 32 (over y, z_lo).
Axes of the slice: x: 4, y: 8, z: 8 (z_hi: 2, z_lo: 4; z = z_hi * 4 + z_lo), core: 2. Of those that a mesh axis runs over, the one named last changes fastest.
Arguments:
- sensitivity: bfloat16 [2048, 16, 16384], P(None, 'tm', 'cell'), may hold values from -0.25 to 0.25
- duals: bfloat16 [2048, 128], P(('tm', 'cell')), may hold values from -6 to 6
- time_cov: float32 [16, 16], replicated, may hold values from 0.05 to 0.5
- cell_coords: int32 [2, 16384], P(None, 'cell'), may hold values from 0 to 127, as said below
- obs_time: int32 [2048], replicated, may hold values from 0 to 15
- obs_owner: int32 [2048], replicated, may hold values from 0 to 2047, each once
Outputs:
- product: float32 [2048, 128], P(('tm', 'cell'))
Inputs may be any that keep to these rules, and one draw needn't show every extreme that they name: `cell_coords`: every cell has its own grid position; rows lie below 128 and columns below 128. `obs_owner`: every observation stands in exactly one slot.
All inputs are finite; a program needn't handle non-finite values.
Results may differ from a plain program's by a relative error of at most 0.0049.
Values may be sent and summed in bfloat16 or wider, within the bound.
No kernel may reach another device: no remote copies, remote signals or barrier semaphores. Data moves between devices by JAX's collectives and lax.ppermute only.
A program may use at most 64 MiB of HBM per device.

v0:
```python
import jax
import jax.numpy as jnp
from jax import lax
from jax.sharding import Mesh
from jax.sharding import PartitionSpec as P

LSCALE = 4
TM = ("tm_0", "tm_1", "tm_2")
TM_CELL = ("tm_0", "tm_1", "tm_2", "cell_0", "cell_1")
CELL = ("cell_0", "cell_1")


def laid_out(pieces, dim):
    pieces = jnp.moveaxis(pieces, 0, dim)
    shape = pieces.shape
    return pieces.reshape(*shape[:dim], shape[dim] * shape[dim + 1], *shape[dim + 2 :])


def sent_to_all(array, axis):
    copies = jnp.broadcast_to(array, (lax.axis_size(axis), *array.shape))
    return lax.all_to_all(copies, axis, split_axis=0, concat_axis=0, tiled=True)


def gathered_copies(array, axis, dim):
    return laid_out(sent_to_all(array, axis), dim)


def cut_along(array, dim, length):
    shape = array.shape
    pieces = array.reshape(*shape[:dim], length, shape[dim] // length, *shape[dim + 1 :])
    return jnp.moveaxis(pieces, dim, 0)


def edges_of(length, count):
    hop = length // count
    if hop >= 8:
        hop -= hop % 8
    return [hop * k for k in range(1, count)]


def own_block(pieces, axes, sequence):
    inside = pieces.shape[1:]
    pieces = pieces.reshape(*(lax.axis_size(a) for a in axes), *inside)
    pieces = jnp.moveaxis(pieces, sequence, range(len(axes))).reshape(-1, *inside)
    for k in sequence:
        pieces = lax.psum_scatter(pieces, axes[k], scatter_dimension=0, tiled=True)
    return pieces[0]


def sum_at_once(array, axes, dim):
    pieces = cut_along(array, dim, lax.axis_size(axes))
    widest = max(range(1, max(2, pieces.ndim - 1)), key=lambda d: pieces.shape[d])
    count, done = (len(axes), [])
    for first, slab in enumerate(
        jnp.split(pieces, edges_of(pieces.shape[widest], count), axis=widest)
    ):
        if slab.size:
            sequence = [(first + k) % count for k in range(count)]
            done.append(own_block(slab, axes, sequence))
    return jnp.concatenate(done, axis=widest - 1)


def covariance(left_coords, right_coords):
    row_gap = (left_coords[0][:, None] - right_coords[0][None, :]).astype(jnp.float32)
    col_gap = (left_coords[1][:, None] - right_coords[1][None, :]).astype(jnp.float32)
    distance = jnp.sqrt(row_gap * row_gap + col_gap * col_gap)
    return (jnp.exp(-distance / LSCALE) / (8.0 * LSCALE)).astype(jnp.bfloat16)


def per_device(sensitivity, duals, time_cov, cell_coords, obs_time, obs_owner):
    obs_count = sensitivity.shape[0]
    time_count = sensitivity.shape[1]
    cell_count = sensitivity.shape[2]
    real_count = duals.shape[1]
    first_time = lax.axis_index(TM) * time_count
    time_index = first_time + jnp.arange(time_count, dtype=jnp.int32)
    live = time_index[None, :, None] <= obs_time[:, None, None]
    masked = jnp.where(live, sensitivity, jnp.zeros((), jnp.bfloat16))
    flattened = masked.reshape(obs_count, time_count * cell_count)
    picked = flattened
    adjoint = lax.dot_general(
        picked,
        lax.all_gather(duals, TM_CELL, axis=0, tiled=True),
        (((0,), (0,)), ((), ())),
        preferred_element_type=jnp.float32,
    )
    local_adj = (
        adjoint.astype(jnp.bfloat16).reshape(time_count, cell_count, real_count).transpose(1, 0, 2)
    )
    all_coords = gathered_copies(cell_coords, CELL, 1)
    spread_adj = lax.all_to_all(local_adj, TM, split_axis=2, concat_axis=1, tiled=True)
    values = jnp.einsum(
        "st,ctr->csr", time_cov, spread_adj.astype(jnp.float32), precision=lax.Precision.HIGHEST
    ).astype(jnp.bfloat16)
    portion = lax.all_gather(values, CELL, axis=0, tiled=True)
    kernel = covariance(cell_coords, all_coords)
    summed = jnp.dot(
        kernel, portion.reshape(portion.shape[0], -1), preferred_element_type=jnp.float32
    )
    weighted = lax.all_to_all(
        summed.reshape(values.shape).astype(jnp.bfloat16),
        TM,
        split_axis=1,
        concat_axis=2,
        tiled=True,
    )
    weighted_flat = weighted.transpose(1, 0, 2).reshape(time_count * cell_count, real_count)
    picked = jnp.take(flattened, obs_owner, axis=0)
    return sum_at_once(
        jnp.dot(picked, weighted_flat, preferred_element_type=jnp.float32), TM_CELL, 0
    )


def solution(mesh):
    split = Mesh(mesh.devices.reshape(4, 2, 2, 8, 4), ("tm_0", "tm_1", "tm_2", "cell_0", "cell_1"))
    return jax.shard_map(
        per_device,
        mesh=split,
        in_specs=(P(None, TM, CELL), P(TM_CELL, None), P(), P(None, CELL), P(), P()),
        out_specs=P(TM_CELL, None),
        check_vma=False,
    )
```

profile of v0, /device:TPU:2, one launch (start us, length us, event | category | flops | bytes accessed | tf_op | source)
XLA Modules:
  0.0 1611.9 jit_solution(16433688849147574105)
XLA Ops:
  6.5 1138.5 %all-gather = bf16[512,4,128]{2,1,0:T(4,128)(2,1)S(1)} all-gather(bf16[1,4,128]{2,1,0:T(4,128)(2,1)} %bitcast.57), channel_id=1, replica_groups=mesh['tm_0'=4,'tm_1'=2,'tm_2'=2,'cell_0'=8,'cell_1'=4] {'tm_0','tm_1','t..., dimensions={0}, use_global_device_ids=true | all-gather | bytes 525312 | tf_op jit(solution)/shard_map/all_gather | solution.py:83
  1145.0 0.7 broadcast_compare_fusion
  1145.7 1.8 select_bitcast_fusion
  1147.5 0.8 fusion.14
  1148.3 0.2 copy.17
  1148.5 0.5 broadcast.41
  1149.0 1.4 reduce
  1150.5 126.0 %all_to_all.26 = bf16[16,2,2048]{2,1,0:T(2,128)(2,1)S(1)} all-to-all(bf16[16,2,2048]{2,1,0:T(2,128)(2,1)S(1)} %reshape.87), channel_id=1, replica_groups=mesh['tm_0'=4,'tm_1'=2,'tm_2'=2,'cell_0'=8,'cell_1'=4] {'tm_0','tm_1','t..., dimensions={0} | all-to-all | bytes 262144 | tf_op jit(solution)/shard_map/all_to_all | solution.py:91
  1276.5 0.1 reshape.88
  1276.7 0.9 fusion.15
  1277.6 0.7 broadcast_in_dim.33
  1278.3 3.9 all-to-all-start
  1282.2 9.2 gather_fusion
  1291.4 3.9 all-to-all-done
  1295.3 0.1 fusion.22
  1295.4 136.2 %all-gather.3.cloned.1.call-done = bf16[16384,16,8]{0,1,2:T(8,128)(2,1)} async-done(((bf16[512,16,8]{0,1,2:T(8,128)(2,1)}), bf16[16384,16,8]{0,1,2:T(8,128)(2,1)}) %all-gather.3.cloned.1.call-update) | async-done | bytes 4194320 | tf_op jit(solution)/shard_map/all_gather | solution.py:95
  1431.6 22.9 %fusion.9 = bf16[512,16,8]{0,1,2:T(8,128)(2,1)S(1)} fusion(bf16[16384,16,8]{0,1,2:T(8,128)(2,1)} %all-gather.3.cloned.1.call-done, s32[16384]{0:T(1024)S(1)} %bitcast.54, s32[512]{0:T(512)S(1)} %bitcast.56, s32[16384]{0:T(1024)S(1)} %bitcast.53, s32[512]{0:T(512)S(1)} %bitcast.55), kind=kOutput, calls=%fused_computation.12 | convolution fusion | flops 2239823872 | bytes 4460544 | tf_op jit(solution)/shard_map/dot_general | solution.py:97
  1454.5 0.7 copy.21
  1455.3 7.0 all-to-all-start.2
  1462.3 1.6 broadcast_select_fusion
  1463.9 2.5 select_n.30
  1466.4 4.6 all-to-all-done.2
  1471.0 1.3 fusion.6
  1472.3 1.1 copy.24
  1473.5 32.9 %reduce-scatter.5.cloned.1.call-done = f32[128,4,128]{2,0,1:T(8,128)} async-done(((f32[512,4,128]{2,0,1:T(8,128)}), f32[128,4,128]{2,0,1:T(8,128)}) %reduce-scatter.5.cloned.1.call-update) | async-done | bytes 262160 | tf_op jit(solution)/shard_map/reduce_scatter | solution.py:46
  1506.5 26.7 %reduce-scatter.7.cloned.1.call-done = f32[32,4,128]{2,0,1:T(8,128)} async-done(((f32[128,4,128]{2,0,1:T(8,128)}), f32[32,4,128]{2,0,1:T(8,128)}) %reduce-scatter.7.cloned.1.call-update) | async-done | bytes 65552 | tf_op jit(solution)/shard_map/reduce_scatter | solution.py:46
  1533.2 26.2 %reduce-scatter.9.cloned.1.call-done = f32[16,4,128]{2,0,1:T(8,128)} async-done(((f32[32,4,128]{2,0,1:T(8,128)}), f32[16,4,128]{2,0,1:T(8,128)}) %reduce-scatter.9.cloned.1.call-update) | async-done | bytes 32784 | tf_op jit(solution)/shard_map/reduce_scatter | solution.py:46
  1559.4 1.3 dynamic-slice
  1560.8 12.9 reduce-scatter.11.cloned.1.call-done
  1573.7 0.7 copy.25
  1574.4 29.7 %all-reduce = f32[8,4,128]{2,1,0:T(4,128)S(1)} all-reduce(f32[8,4,128]{2,1,0:T(4,128)S(1)} %copy.25), channel_id=6, replica_groups=mesh['tm_0'=4,'tm_1'=2,'tm_2'=2,'cell_0'=8,'cell_1'=4] {'cell_0'}, use_global_device_ids=true, to_apply=%region_4.5.clone | all-reduce | flops 4096 | bytes 32768
  1604.1 1.3 dynamic-slice_bitcast_fusion
  (23 shorter events, 0.4 us)
Async XLA Ops:
  6.5 1270.1 %copy-start = (f32[16,16]{1,0:T(8,128)S(1)}, f32[16,16]{1,0:T(8,128)}, u32[]{:S(2)}) copy-start(f32[16,16]{1,0:T(8,128)} %param.8) | copy-start | bytes 3076
  6.5 1425.1 %all-gather.3.cloned.1.call-start = ((), (), s32[]{:S(2)}) async-start(), calls=%async_computation.7 | async-start | bytes 4325376 | tf_op jit(solution)/shard_map/all_gather | solution.py:95
  1145.7 131.9 %copy-start.3 = (s32[2,512]{1,0:T(2,128)S(1)}, s32[2,512]{1,0:T(2,128)}, u32[]{:S(2)}) copy-start(s32[2,512]{1,0:T(2,128)} %param.9) | copy-start | bytes 12292
  1145.7 136.4 %copy-start.2 = (s32[2048]{0:T(1024)S(1)}, s32[2048]{0:T(1024)}, u32[]{:S(2)}) copy-start(s32[2048]{0:T(1024)} %param.11) | copy-start | bytes 24580
  1278.3 17.0 %all-to-all-start = ((s32[32,2,512]{2,1,0:T(2,128)}), s32[32,2,512]{2,1,0:T(2,128)S(1)}, u32[]{:S(2)}, u32[]{:S(2)}) async-start(s32[32,2,512]{2,1,0:T(2,128)} %broadcast_in_dim.33), calls=%async_computation | async-start | bytes 262144 | tf_op jit(solution)/shard_map/all_to_all | solution.py:21
  1431.6 30.7 %copy-start.1 = (bf16[2048,512]{1,0:T(8,128)(2,1)S(1)}, bf16[2048,512]{1,0:T(8,128)(2,1)}, u32[]{:S(2)}) copy-start(bf16[2048,512]{1,0:T(8,128)(2,1)} %gather_fusion) | copy-start | bytes 6291460
  1455.3 15.8 all-to-all-start.2
  1462.2 44.2 %reduce-scatter.5.cloned.1.call-start = ((), (), s32[]{:S(2)}) async-start(), calls=%async_computation.8 | async-start | bytes 1310720 | tf_op jit(solution)/shard_map/reduce_scatter | solution.py:46
  1473.5 59.7 %reduce-scatter.7.cloned.1.call-start = ((), (), s32[]{:S(2)}) async-start(), calls=%async_computation.9 | async-start | bytes 327680 | tf_op jit(solution)/shard_map/reduce_scatter | solution.py:46
  1506.5 52.9 %reduce-scatter.9.cloned.1.call-start = ((), (), s32[]{:S(2)}) async-start(), calls=%async_computation.10 | async-start | bytes 98304 | tf_op jit(solution)/shard_map/reduce_scatter | solution.py:46
  1533.2 40.5 %reduce-scatter.11.cloned.1.call-start = ((), (), s32[]{:S(2)}) async-start(), calls=%async_computation.11 | async-start | bytes 49152 | tf_op jit(solution)/shard_map/reduce_scatter | solution.py:46
Sparse Core Ops, SparseCore 0:
  1277.7 153.8 all-gather.2
  1473.6 32.7 reduce-scatter.4
  1509.5 23.6 reduce-scatter.6
  1535.8 23.5 reduce-scatter.8
  1562.0 11.6 reduce-scatter.10
where the time goes:
time: 1610 us
  blocking collectives  1290 us (80%)
  waiting for transfers between devices  243 us (15%)
  matrix products  25.9 us (2%)
  local copies, waits for them, and re-layouts  18.6 us (1%)
    all_gather x1, blocking collectives, per_device(): lax.all_gather(duals, TM_CELL, axis=0, tiled=True)  1140 us
    all_gather x1, waiting for transfers between devices, per_device(): portion = lax.all_gather(values, CELL, axis=0, tiled=True)  136 us
    all_to_all x1, blocking collectives, per_device(): lax.all_to_all(local_adj, TM, split_axis=2, concat_axis=1, tiled=True)  126 us
    reduce_scatter x4, waiting for transfers between devices, own_block(): pieces = lax.psum_scatter(pieces, axes[k], scatter_dimension=0, tiled=True)  98.7 us
  transfers between devices with their start and end apart: 7, of which 7 were waited for; matrix products, arithmetic and copies ran while one was open for 1% of the time, Pallas kernels for 0%

commit v1 on v0

--- a/solution.py
+++ b/solution.py
@@ -8,6 +8,11 @@
 TM = ("tm_0", "tm_1", "tm_2")
 TM_CELL = ("tm_0", "tm_1", "tm_2", "cell_0", "cell_1")
 CELL = ("cell_0", "cell_1")
+
+
+def gather_over(x, axis, dim):
+    repeated = jnp.stack([x] * lax.axis_size(axis))
+    return jnp.concatenate(lax.all_to_all(repeated, axis, 0, 0), axis=dim)
 
 
 def laid_out(pieces, dim):
@@ -80,7 +85,7 @@
     picked = flattened
     adjoint = lax.dot_general(
         picked,
-        lax.all_gather(duals, TM_CELL, axis=0, tiled=True),
+        gather_over(duals, TM_CELL, 0),
         (((0,), (0,)), ((), ())),
         preferred_element_type=jnp.float32,
     )

time: 1610 us -> 405 us (0.25)
  blocking collectives: 1290 us -> 43.6 us
  waiting for transfers between devices: 243 us -> 264 us
  starting transfers between devices: 11 us -> 31.9 us
    all_gather x1 -> x0, blocking collectives: 1140 us -> none  [per_device(): lax.all_gather(duals, TM_CELL, axis=0, tiled=True)]
    all_to_all x1, blocking collectives: 126 us -> 13.9 us  [per_device(): lax.all_to_all(local_adj, TM, split_axis=2, concat_axis=1, tiled=True)]
    all_to_all x0 -> x1, starting transfers between devices: none -> 21.2 us  [gather_over(): return jnp.concatenate(lax.all_to_all(repeated, axis, 0, 0), axis=dim)]
    all_to_all x0 -> x1, waiting for transfers between devices: none -> 19.2 us  [gather_over(): return jnp.concatenate(lax.all_to_all(repeated, axis, 0, 0), axis=dim)]
  transfers between devices with their start and end apart: 7 -> 8, of which waited for: 7 -> 8; matrix products, arithmetic and copies ran while one was open for 1% -> 4% of each run, Pallas kernels for 0% -> 0%
where the time goes in v1:
time: 405 us; the launch traced here: 404 us
  waiting for transfers between devices  264 us (65%)
  blocking collectives  43.6 us (11%)
  starting transfers between devices  31.9 us (8%)
  matrix products  25.9 us (6%)
  local copies, waits for them, and re-layouts  20.1 us (5%)
  between operations  13.3 us (3%)
  other arithmetic  5.5 us (1%)
    all_gather x1, waiting for transfers between devices, per_device(): portion = lax.all_gather(values, CELL, axis=0, tiled=True)  138 us
    reduce_scatter x4, waiting for transfers between devices, own_block(): pieces = lax.psum_scatter(pieces, axes[k], scatter_dimension=0, tiled=True)  98.7 us
    unnamed x1, blocking collectives  29.7 us
    dot_general x1, matrix products, per_device(): jnp.dot(kernel, portion.reshape(portion.shape[0], -1), preferred_element_...  22.9 us
    all_to_all x1, starting transfers between devices, gather_over(): return jnp.concatenate(lax.all_to_all(repeated, axis, 0, 0), axis=dim)  21.2 us
    all_to_all x1, waiting for transfers between devices, gather_over(): return jnp.concatenate(lax.all_to_all(repeated, axis, 0, 0), axis=dim)  19.2 us
    all_to_all x1, blocking collectives, per_device(): lax.all_to_all(local_adj, TM, split_axis=2, concat_axis=1, tiled=True)  13.9 us
    gather x1, local copies, waits for them, and re-layouts, per_device(): picked = jnp.take(flattened, obs_owner, axis=0)  9.19 us
  transfers between devices with their start and end apart: 8, of which 8 were waited for; matrix products, arithmetic and copies ran while one was open for 4% of the time, Pallas kernels for 0%

profile of v1, /device:TPU:2, one launch (start us, length us, event | category | flops | bytes accessed | tf_op | source)
XLA Modules:
  0.0 404.2 jit_solution(6892822780598385411)
XLA Ops:
  6.5 1.6 stack.2
  8.2 21.2 %all-to-all-start.1 = ((bf16[512,4,128]{2,1,0:T(4,128)(2,1)}), bf16[512,4,128]{2,1,0:T(4,128)(2,1)S(1)}, u32[]{:S(2)}, u32[]{:S(2)}) async-start(bf16[512,4,128]{2,1,0:T(4,128)(2,1)} %stack.2), calls=%async_computation.1 | async-start | bytes 1048576 | tf_op jit(solution)/shard_map/all_to_all | solution.py:15
  29.4 0.7 broadcast_compare_fusion
  30.1 1.8 select_bitcast_fusion
  31.9 19.2 %all-to-all-done.1 = bf16[512,4,128]{2,1,0:T(4,128)(2,1)S(1)} async-done(((bf16[512,4,128]{2,1,0:T(4,128)(2,1)}), bf16[512,4,128]{2,1,0:T(4,128)(2,1)S(1)}, u32[]{:S(2)}, u32[]{:S(2)}) %all-to-all-start.1) | async-done | bytes 524320 | tf_op jit(solution)/shard_map/all_to_all | solution.py:15
  51.1 0.8 fusion.14
  51.9 0.2 copy.17
  52.1 0.5 broadcast.43
  52.6 1.4 reduce
  54.1 13.9 %all_to_all.31 = bf16[16,2,2048]{2,1,0:T(2,128)(2,1)S(1)} all-to-all(bf16[16,2,2048]{2,1,0:T(2,128)(2,1)S(1)} %reshape.91), channel_id=1, replica_groups=mesh['tm_0'=4,'tm_1'=2,'tm_2'=2,'cell_0'=8,'cell_1'=4] {'tm_0','tm_1','t..., dimensions={0} | all-to-all | bytes 262144 | tf_op jit(solution)/shard_map/all_to_all | solution.py:96
  68.1 0.9 fusion.15
  69.1 0.7 broadcast_in_dim.33
  69.7 4.5 %all-to-all-start = ((s32[32,2,512]{2,1,0:T(2,128)}), s32[32,2,512]{2,1,0:T(2,128)S(1)}, u32[]{:S(2)}, u32[]{:S(2)}) async-start(s32[32,2,512]{2,1,0:T(2,128)} %broadcast_in_dim.33), calls=%async_computation | async-start | bytes 262144 | tf_op jit(solution)/shard_map/all_to_all | solution.py:26
  74.3 9.2 %gather_fusion = bf16[2048,512]{1,0:T(8,128)(2,1)} fusion(bf16[2048,512]{1,0:T(8,128)(2,1)S(1)} %select_bitcast_fusion, s32[2048]{0:T(1024)S(1)} %fusion.19), kind=kCustom, calls=%fused_computation | custom fusion | bytes 4202496 | tf_op jit(solution)/shard_map/jit(_take)/gather | solution.py:113
  83.5 3.4 all-to-all-done
  87.1 137.8 %all-gather.2.cloned.1.call-done = bf16[16384,16,8]{0,1,2:T(8,128)(2,1)} async-done(((bf16[512,16,8]{0,1,2:T(8,128)(2,1)}), bf16[16384,16,8]{0,1,2:T(8,128)(2,1)}) %all-gather.2.cloned.1.call-update) | async-done | bytes 4194320 | tf_op jit(solution)/shard_map/all_gather | solution.py:100
  224.9 22.9 %fusion.9 = bf16[512,16,8]{0,1,2:T(8,128)(2,1)S(1)} fusion(bf16[16384,16,8]{0,1,2:T(8,128)(2,1)} %all-gather.2.cloned.1.call-done, s32[16384]{0:T(1024)S(1)} %bitcast.53, s32[512]{0:T(512)S(1)} %bitcast.55, s32[16384]{0:T(1024)S(1)} %bitcast.52, s32[512]{0:T(512)S(1)} %bitcast.54), kind=kOutput, calls=%fused_computation.12 | convolution fusion | flops 2239823872 | bytes 4460544 | tf_op jit(solution)/shard_map/dot_general | solution.py:102
  247.8 0.7 copy.21
  248.6 6.0 %all-to-all-start.3 = ((bf16[512,16,8]{0,2,1:T(8,128)(2,1)}), bf16[512,16,8]{0,2,1:T(8,128)(2,1)S(1)}, u32[]{:S(2)}, u32[]{:S(2)}) async-start(bf16[512,16,8]{0,2,1:T(8,128)(2,1)} %copy.21), calls=%async_computation.3 | async-start | bytes 262144 | tf_op jit(solution)/shard_map/all_to_all | solution.py:105
  254.6 1.6 broadcast_select_fusion
  256.1 2.5 select_n.30
  258.7 4.6 %all-to-all-done.3 = bf16[512,16,8]{0,2,1:T(8,128)(2,1)S(1)} async-done(((bf16[512,16,8]{0,2,1:T(8,128)(2,1)}), bf16[512,16,8]{0,2,1:T(8,128)(2,1)S(1)}, u32[]{:S(2)}, u32[]{:S(2)}) %all-to-all-start.3) | async-done | bytes 131104 | tf_op jit(solution)/shard_map/all_to_all | solution.py:105
  263.3 1.3 fusion.6
  264.6 1.1 copy.24
  265.8 32.9 %reduce-scatter.5.cloned.1.call-done = f32[128,4,128]{2,0,1:T(8,128)} async-done(((f32[512,4,128]{2,0,1:T(8,128)}), f32[128,4,128]{2,0,1:T(8,128)}) %reduce-scatter.5.cloned.1.call-update) | async-done | bytes 262160 | tf_op jit(solution)/shard_map/reduce_scatter | solution.py:51
  298.8 26.7 %reduce-scatter.7.cloned.1.call-done = f32[32,4,128]{2,0,1:T(8,128)} async-done(((f32[128,4,128]{2,0,1:T(8,128)}), f32[32,4,128]{2,0,1:T(8,128)}) %reduce-scatter.7.cloned.1.call-update) | async-done | bytes 65552 | tf_op jit(solution)/shard_map/reduce_scatter | solution.py:51
  325.5 26.2 %reduce-scatter.9.cloned.1.call-done = f32[16,4,128]{2,0,1:T(8,128)} async-done(((f32[32,4,128]{2,0,1:T(8,128)}), f32[16,4,128]{2,0,1:T(8,128)}) %reduce-scatter.9.cloned.1.call-update) | async-done | bytes 32784 | tf_op jit(solution)/shard_map/reduce_scatter | solution.py:51
  351.7 1.3 dynamic-slice
  353.0 13.0 %reduce-scatter.11.cloned.1.call-done = f32[8,4,128]{2,0,1:T(8,128)} async-done(((f32[16,4,128]{2,0,1:T(8,128)}), f32[8,4,128]{2,0,1:T(8,128)}) %reduce-scatter.11.cloned.1.call-update) | async-done | bytes 16400 | tf_op jit(solution)/shard_map/reduce_scatter | solution.py:51
  366.0 0.7 copy.25
  366.7 29.7 %all-reduce = f32[8,4,128]{2,1,0:T(4,128)S(1)} all-reduce(f32[8,4,128]{2,1,0:T(4,128)S(1)} %copy.25), channel_id=6, replica_groups=mesh['tm_0'=4,'tm_1'=2,'tm_2'=2,'cell_0'=8,'cell_1'=4] {'cell_0'}, use_global_device_ids=true, to_apply=%region_4.5.clone | all-reduce | flops 4096 | bytes 32768
  396.4 1.2 dynamic-slice_bitcast_fusion
  (25 shorter events, 0.6 us)
Async XLA Ops:
  6.5 61.6 %copy-start = (f32[16,16]{1,0:T(8,128)S(1)}, f32[16,16]{1,0:T(8,128)}, u32[]{:S(2)}) copy-start(f32[16,16]{1,0:T(8,128)} %param.8) | copy-start | bytes 3076
  8.2 42.9 %all-to-all-start.1 = ((bf16[512,4,128]{2,1,0:T(4,128)(2,1)}), bf16[512,4,128]{2,1,0:T(4,128)(2,1)S(1)}, u32[]{:S(2)}, u32[]{:S(2)}) async-start(bf16[512,4,128]{2,1,0:T(4,128)(2,1)} %stack.2), calls=%async_computation.1 | async-start | bytes 1048576 | tf_op jit(solution)/shard_map/all_to_all | solution.py:15
  29.4 195.5 %all-gather.2.cloned.1.call-start = ((), (), s32[]{:S(2)}) async-start(), calls=%async_computation.8 | async-start | bytes 4325376 | tf_op jit(solution)/shard_map/all_gather | solution.py:100
  30.1 38.9 %copy-start.3 = (s32[2,512]{1,0:T(2,128)S(1)}, s32[2,512]{1,0:T(2,128)}, u32[]{:S(2)}) copy-start(s32[2,512]{1,0:T(2,128)} %param.9) | copy-start | bytes 12292
  30.1 44.2 %copy-start.2 = (s32[2048]{0:T(1024)S(1)}, s32[2048]{0:T(1024)}, u32[]{:S(2)}) copy-start(s32[2048]{0:T(1024)} %param.11) | copy-start | bytes 24580
  69.7 17.2 %all-to-all-start = ((s32[32,2,512]{2,1,0:T(2,128)}), s32[32,2,512]{2,1,0:T(2,128)S(1)}, u32[]{:S(2)}, u32[]{:S(2)}) async-start(s32[32,2,512]{2,1,0:T(2,128)} %broadcast_in_dim.33), calls=%async_computation | async-start | bytes 262144 | tf_op jit(solution)/shard_map/all_to_all | solution.py:26
  224.9 29.7 %copy-start.1 = (bf16[2048,512]{1,0:T(8,128)(2,1)S(1)}, bf16[2048,512]{1,0:T(8,128)(2,1)}, u32[]{:S(2)}) copy-start(bf16[2048,512]{1,0:T(8,128)(2,1)} %gather_fusion) | copy-start | bytes 6291460
  248.6 14.8 %all-to-all-start.3 = ((bf16[512,16,8]{0,2,1:T(8,128)(2,1)}), bf16[512,16,8]{0,2,1:T(8,128)(2,1)S(1)}, u32[]{:S(2)}, u32[]{:S(2)}) async-start(bf16[512,16,8]{0,2,1:T(8,128)(2,1)} %copy.21), calls=%async_computation.3 | async-start | bytes 262144 | tf_op jit(solution)/shard_map/all_to_all | solution.py:105
  254.5 44.2 %reduce-scatter.5.cloned.1.call-start = ((), (), s32[]{:S(2)}) async-start(), calls=%async_computation.9 | async-start | bytes 1310720 | tf_op jit(solution)/shard_map/reduce_scatter | solution.py:51
  265.8 59.7 %reduce-scatter.7.cloned.1.call-start = ((), (), s32[]{:S(2)}) async-start(), calls=%async_computation.10 | async-start | bytes 327680 | tf_op jit(solution)/shard_map/reduce_scatter | solution.py:51
  298.7 53.0 %reduce-scatter.9.cloned.1.call-start = ((), (), s32[]{:S(2)}) async-start(), calls=%async_computation.11 | async-start | bytes 98304 | tf_op jit(solution)/shard_map/reduce_scatter | solution.py:51
  325.5 40.5 %reduce-scatter.11.cloned.1.call-start = ((), (), s32[]{:S(2)}) async-start(), calls=%async_computation.12 | async-start | bytes 49152 | tf_op jit(solution)/shard_map/reduce_scatter | solution.py:51
Sparse Core Ops, SparseCore 0:
  69.2 155.6 all-gather.1
  265.9 32.7 reduce-scatter.4
  301.7 23.6 reduce-scatter.6
  328.0 23.6 reduce-scatter.8
  354.3 11.6 reduce-scatter.10
